TPU v7x, 256 devices: a whole 4x4x8 slice. The times are simulated.
256 devices in a mesh: acq: 4 (over x), tile: 64 (over z, y, core).
Axes of the slice: x: 4, y: 4, z: 8, core: 2. Of those that a mesh axis runs over, the one named last changes fastest.
Arguments:
- slc: bfloat16 [16, 2, 8192, 1280], P('acq', None, 'tile')
- match: int32 [2, 16], replicated, may hold values from 0 to 3, as said below
- dest: int32 [64, 16, 32, 1], P('tile', 'acq'), may hold values from 0 to 3; in each aligned block of 128 rows (0 to 127, 128 to 255, ..., all dimensions but the last counted through in order) at most 64 rows name the same one
- coherent: int32 [64, 16, 32], P('tile', 'acq'), may hold values 0 or 1
Outputs:
- received: bfloat16 [64, 1024, 2, 128], P('tile', 'acq')
Inputs may be any that keep to these rules, and one draw needn't show every extreme that they name: `match`: within each round, the entries of each aligned run of 4 acquisitions are a permutation of 0 to 3. `dest`: among the 128 rows of one device, at most 64 name the same owner.
All inputs are finite; a program needn't handle non-finite values. No bound on the sum of `coherent` on one device may be relied on, other than what follows from the above.
Results may differ from a plain program's by a relative error of at most 0.001.
Values may be sent and summed in bfloat16 or wider, within the bound.
No kernel may reach another device: no remote copies, remote signals or barrier semaphores. Data moves between devices by JAX's collectives and lax.ppermute only.
A program may use at most 128 MiB of HBM per device.

v0:
```python
import jax
import jax.numpy as jnp
from jax import lax
from jax.sharding import PartitionSpec as P

PATCH = 32
LOOK_L = 4
LOOK_S = 20
BLOCK_ROWS = 4
ROUNDS = 2
power_floor = 0.25
energy_eps = 1e-06


def swapped(x, axis, stride):
    return lax.ppermute(x, axis, [(i, i ^ 1 << stride) for i in range(lax.axis_size(axis))])


def dft_tables():
    counter = jnp.arange(PATCH)
    phase = counter[:, None] * counter[None, :] % PATCH
    angle = phase.astype(jnp.float32) * (2.0 * 3.141592653589793 / PATCH)
    return (jnp.cos(angle), jnp.sin(angle))


def along_axes(real_part, imag_part, cosine, sine_tab, sign, form):
    hold = lax.Precision.HIGHEST
    c_real = jnp.einsum(form, cosine, real_part, precision=hold)
    c_imag = jnp.einsum(form, cosine, imag_part, precision=hold)
    s_real = jnp.einsum(form, sine_tab, real_part, precision=hold)
    s_imag = jnp.einsum(form, sine_tab, imag_part, precision=hold)
    return (c_real - sign * s_imag, c_imag + sign * s_real)


def transform(real_part, imag_part, cosine, sine_tab, sign):
    real_part, imag_part = along_axes(
        real_part, imag_part, cosine, sine_tab, sign, "jk,aPkQl->aPjQl"
    )
    return along_axes(real_part, imag_part, cosine, sine_tab, sign, "lm,aPkQm->aPkQl")


def cross_looks(left, right, picks):
    acq_dev, _, line_count, sample_count = left.shape
    other = jnp.take(right, picks, axis=0)
    own_real = left[:, 0].astype(jnp.float32)
    own_imag = left[:, 1].astype(jnp.float32)
    other_real = other[:, 0].astype(jnp.float32)
    other_imag = other[:, 1].astype(jnp.float32)
    real_part = own_real * other_real + own_imag * other_imag
    imag_part = own_imag * other_real - own_real * other_imag
    stacked = jnp.stack([real_part, imag_part], axis=1)
    stacked = stacked.reshape(
        acq_dev, 2, line_count // LOOK_L, LOOK_L, sample_count // LOOK_S, LOOK_S
    )
    return jnp.sum(stacked, axis=(3, 5)) / (LOOK_L * LOOK_S)


def shards(slc, match, dest, coherent):
    acq_dev, _, lines_dev, samples_dev = slc.shape
    n_acq = lax.axis_size("acq")
    n_tile = lax.axis_size("tile")
    far_bit = n_acq.bit_length() - 2
    grid_count = lines_dev * n_tile // LOOK_L * (samples_dev // LOOK_S)
    patch_rows = lines_dev // LOOK_L // PATCH
    patch_cols = samples_dev // LOOK_S // PATCH
    cosine, sine_tab = dft_tables()
    my_group = lax.axis_index("acq")

    def swap_tiles(tiles, round_number):
        if round_number == 0:
            return swapped(tiles, "acq", 0)
        return swapped(tiles, "acq", far_bit)

    order_list = [0, 1]
    looked_all = {}
    filtered_all = {}
    for round_number in order_list:
        own_match = lax.dynamic_slice_in_dim(match[round_number], my_group * acq_dev, acq_dev)
        group_tiles = swap_tiles(slc, round_number)
        looked_all[round_number] = cross_looks(slc, group_tiles, own_match)
        local_looked = looked_all[round_number]
        total = lax.psum(
            jnp.sum(local_looked[:, 0] ** 2 + local_looked[:, 1] ** 2, axis=(1, 2)), "tile"
        )
        energy = total / grid_count + energy_eps
        looked = looked_all[round_number]
        shape_six = (acq_dev, patch_rows, PATCH, patch_cols, PATCH)
        real_part = looked[:, 0].reshape(shape_six)
        imag_part = looked[:, 1].reshape(shape_six)
        spec_real, spec_imag = transform(real_part, imag_part, cosine, sine_tab, -1.0)
        scale = energy[:, None, None, None, None]
        power = (spec_real**2 + spec_imag**2) / (PATCH * PATCH * scale)
        weight = (power + power_floor) ** 0.25
        back_real, back_imag = transform(
            weight * spec_real, weight * spec_imag, cosine, sine_tab, 1.0
        )
        norm_factor = 1.0 / (PATCH * PATCH * jnp.sqrt(scale))
        parts = jnp.stack([back_real * norm_factor, back_imag * norm_factor], axis=-1)
        parts = parts.reshape(
            acq_dev, patch_rows, PATCH // BLOCK_ROWS, BLOCK_ROWS, patch_cols, PATCH, 2
        )
        parts = jnp.transpose(parts, (0, 1, 2, 4, 6, 3, 5))
        filtered_all[round_number] = parts.reshape(
            acq_dev, patch_rows * (PATCH // BLOCK_ROWS) * patch_cols, 2, BLOCK_ROWS * PATCH
        )
    stacked = jnp.stack([filtered_all[round_number] for round_number in range(ROUNDS)], axis=1)
    block_len = BLOCK_ROWS * PATCH
    rows_dev = stacked.shape[0] * stacked.shape[1] * stacked.shape[2]
    cap_rows = max(3, 2 * ((rows_dev + n_acq - 1) // n_acq))
    stacked = stacked.reshape(rows_dev, 2, block_len)
    mask_rows = coherent.reshape(rows_dev).astype(jnp.float32)
    value = (stacked * mask_rows[:, None, None]).astype(jnp.bfloat16)
    owner = dest.reshape(rows_dev)
    onehot = (owner[:, None] == jnp.arange(n_acq)).astype(jnp.int32)
    rank = jnp.sum((jnp.cumsum(onehot, axis=0) - onehot) * onehot, axis=1)
    hits = (onehot[:, :, None] == 1) & (rank[:, None, None] == jnp.arange(cap_rows)[None, None, :])
    select = hits.astype(jnp.bfloat16).reshape(rows_dev, n_acq * cap_rows)
    outgoing = jnp.einsum("ks,kcp->scp", select, value, preferred_element_type=jnp.float32).astype(
        jnp.bfloat16
    )
    incoming = lax.all_to_all(outgoing, "acq", split_axis=0, concat_axis=0, tiled=True)
    return incoming[None]


def solution(mesh):
    return jax.shard_map(
        shards,
        mesh=mesh,
        in_specs=(
            P("acq", None, "tile", None),
            P(),
            P("tile", "acq", None, None),
            P("tile", "acq", None),
        ),
        out_specs=P("tile", "acq", None, None),
        check_vma=False,
    )
```

profile of v0, /device:TPU:2, one launch (start us, length us, event | category | flops | bytes accessed | tf_op | source)
XLA Modules:
  0.0 392.0 jit_solution(11845834372850043596)
XLA Ops:
  0.0 2.1 collective-permute-start.1
  2.1 1.4 collective-permute-start
  3.6 0.7 convert_element_type.142
  4.3 0.5 broadcast.327
  4.8 1.3 reduce.5
  6.6 0.8 fusion.240
  7.8 53.8 %collective-permute-done.1 = bf16[4,2,128,1280]{3,2,1,0:T(8,128)(2,1)} collective-permute-done((bf16[4,2,128,1280]{3,2,1,0:T(8,128)(2,1)}, bf16[4,2,128,1280]{3,2,1,0:T(8,128)(2,1)}, u32[]{:S(2)}, u32[]{:S(2)}) %collective-permute-start.1) | collective-permute-done | bytes 2621472 | tf_op jit(solution)/shard_map/ppermute | solution.py:16
  61.6 2.5 gather_fusion.1
  64.0 1.8 broadcast_select_fusion
  65.9 50.8 %collective-permute-done = bf16[4,2,128,1280]{3,2,1,0:T(8,128)(2,1)} collective-permute-done((bf16[4,2,128,1280]{3,2,1,0:T(8,128)(2,1)}, bf16[4,2,128,1280]{3,2,1,0:T(8,128)(2,1)}, u32[]{:S(2)}, u32[]{:S(2)}) %collective-permute-start) | collective-permute-done | bytes 2621472 | tf_op jit(solution)/shard_map/ppermute | solution.py:16
  116.6 2.5 gather_fusion
  119.4 1.4 copy-done
  120.8 0.8 copy-done.1
  121.6 4.0 %fusion = (f32[4,1,128,1280]{3,2,1,0:T(8,128)}, f32[4,1,128,1280]{3,2,1,0:T(8,128)}, f32[4,1,128,1280]{3,2,1,0:T(8,128)S(1)}, f32[4,1,128,1280]{3,2,1,0:T(8,128)}) fusion(bf16[4,2,128,1280]{3,2,1,0:T(8,128)(2,1)S(1)} %broadcast_select_fusion.1, bf16[4,2,128,1280]{3,2,1,0:T(8,128)(2,1)S(1)} %copy-done.1, bf16[4,2,128,1280]{3,2,1,0:T(8,128)(2,1)S(1)} %copy-done), kind=kLoop, calls=%fused_computation.12 | loop fusion | flops 11796480 | bytes 18350080 | tf_op jit(solution)/shard_map/add | solution.py:49
  125.6 21.7 %stack.39 = f32[4,1,32,4,64,20]{5,4,3,2,0,1:T(8,128)} reshape(f32[4,1,128,1280]{3,2,1,0:T(8,128)} %get-tuple-element.12) | data formatting | bytes 5242880 | tf_op jit(solution)/shard_map/stack | solution.py:51
  147.3 21.7 %stack.40 = f32[4,1,32,4,64,20]{5,4,3,2,0,1:T(8,128)} reshape(f32[4,1,128,1280]{3,2,1,0:T(8,128)} %get-tuple-element.13) | data formatting | bytes 5242880 | tf_op jit(solution)/shard_map/stack | solution.py:51
  168.9 12.7 %maximum_reduce_fusion = f32[4,2,32,64]{3,2,0,1:T(8,128)S(1)} fusion(f32[4,1,32,4,64,20]{5,4,3,2,0,1:T(8,128)} %stack.40, f32[4,1,32,4,64,20]{5,4,3,2,0,1:T(8,128)} %stack.39), kind=kLoop, calls=%fused_computation.2 | loop fusion | flops 2605056 | bytes 5308416 | tf_op jit(solution)/shard_map/reduce_sum | solution.py:55
  185.0 21.7 %stack.45 = f32[4,1,32,4,64,20]{5,4,3,2,0,1:T(8,128)} reshape(f32[4,1,128,1280]{3,2,1,0:T(8,128)} %get-tuple-element.17) | data formatting | bytes 5242880 | tf_op jit(solution)/shard_map/stack | solution.py:51
  206.7 20.9 %stack.46 = f32[4,1,32,4,64,20]{5,4,3,2,0,1:T(8,128)} reshape(f32[4,1,128,1280]{3,2,1,0:T(8,128)S(1)} %get-tuple-element.16) | data formatting | bytes 5242880 | tf_op jit(solution)/shard_map/stack | solution.py:51
  227.6 12.7 %maximum_reduce_fusion.1 = f32[4,2,32,64]{3,2,0,1:T(8,128)S(1)} fusion(f32[4,1,32,4,64,20]{5,4,3,2,0,1:T(8,128)} %stack.46, f32[4,1,32,4,64,20]{5,4,3,2,0,1:T(8,128)} %stack.45), kind=kLoop, calls=%fused_computation.3 | loop fusion | flops 2605056 | bytes 5308416 | tf_op jit(solution)/shard_map/reduce_sum | solution.py:55
  240.5 131.1 %all-reduce = (f32[4]{0:T(128)S(1)}, f32[4]{0:T(128)S(1)}) all-reduce(f32[4]{0:T(128)S(1)} %get-tuple-element.21, f32[4]{0:T(128)S(1)} %get-tuple-element.19), channel_id=1, replica_groups=mesh['acq'=4,'tile'=64] {'tile'}, use_global_device_ids=true, to_apply=%region_7.9 | all-reduce | flops 8 | bytes 64 | tf_op jit(solution)/shard_map/psum | solution.py:82
  371.6 0.5 fusion.60
  372.1 0.5 fusion.56
  375.8 0.5 fusion.48
  376.3 0.5 fusion.44
  376.9 0.5 fusion.9
  377.8 0.5 fusion.8
  379.1 0.4 fusion.13
  379.8 0.5 fusion.5
  380.7 0.5 fusion.4
  383.1 8.2 %all_to_all.5 = bf16[256,2,128]{2,1,0:T(2,128)(2,1)S(1)} all-to-all(bf16[256,2,128]{2,1,0:T(2,128)(2,1)S(1)} %copy.171), channel_id=1, replica_groups=mesh['acq'=4,'tile'=64] {'acq'}, dimensions={0} | all-to-all | bytes 262144 | tf_op jit(solution)/shard_map/all_to_all | solution.py:121
  391.3 0.7 copy.205
  (56 shorter events, 11.4 us)
Async XLA Ops:
  0.0 61.6 %collective-permute-start.1 = (bf16[4,2,128,1280]{3,2,1,0:T(8,128)(2,1)}, bf16[4,2,128,1280]{3,2,1,0:T(8,128)(2,1)}, u32[]{:S(2)}, u32[]{:S(2)}) collective-permute-start(bf16[4,2,128,1280]{3,2,1,0:T(8,128)(2,1)} %param.6), channel_id=1, source_target_pairs={{0,128},{64,192},{128,0},{192,64},{1,129},{65,193},{129,1},{193,65... | collective-permute-start | bytes 7864328 | tf_op jit(solution)/shard_map/ppermute | solution.py:16
  2.1 114.5 %collective-permute-start = (bf16[4,2,128,1280]{3,2,1,0:T(8,128)(2,1)}, bf16[4,2,128,1280]{3,2,1,0:T(8,128)(2,1)}, u32[]{:S(2)}, u32[]{:S(2)}) collective-permute-start(bf16[4,2,128,1280]{3,2,1,0:T(8,128)(2,1)} %param.6), channel_id=1, source_target_pairs={{0,64},{64,0},{128,192},{192,128},{1,65},{65,1},{129,193},{193,129... | collective-permute-start | bytes 7864328 | tf_op jit(solution)/shard_map/ppermute | solution.py:16
  119.1 1.7 copy-start
  119.1 2.5 copy-start.1
where the time goes:
time: 392 us
  blocking collectives  139 us (35%)
  waiting for transfers between devices  105 us (27%)
  local copies, waits for them, and re-layouts  96 us (24%)
  other arithmetic  34.8 us (9%)
  matrix products  13.3 us (3%)
    psum x1, blocking collectives, shards(): lax.psum(jnp.sum(local_looked[:, 0] ** 2 + local_looked[:, 1] ** 2, axis=...  131 us
    ppermute x2, waiting for transfers between devices, swapped(): lax.ppermute(x, axis, [(i, i ^ 1 << stride) for i in range(lax.axis_size(...  105 us
    another operation x4, local copies, waits for them, and re-layouts, cross_looks(): stacked = jnp.stack([real_part, imag_part], axis=1)  85.9 us
    reduce_sum x2, other arithmetic, cross_looks(): return jnp.sum(stacked, axis=(3, 5)) / (LOOK_L * LOOK_S)  25.5 us
    all_to_all x1, blocking collectives, shards(): lax.all_to_all(outgoing, 'acq', split_axis=0, concat_axis=0, tiled=True)  8.18 us
  transfers between devices with their start and end apart: 2, of which 2 were waited for; matrix products, arithmetic and copies ran while one was open for 2% of the time, Pallas kernels for 0%

commit v1 on v0

--- a/solution.py
+++ b/solution.py
@@ -10,6 +10,28 @@
 ROUNDS = 2
 power_floor = 0.25
 energy_eps = 1e-06
+
+
+def in_blocks(x, dim, devices):
+    before, after = (x.shape[:dim], x.shape[dim + 1 :])
+    return jnp.moveaxis(x.reshape(*before, devices, -1, *after), dim, 0)
+
+
+def in_order(blocks, dim):
+    blocks = jnp.moveaxis(blocks, 0, dim)
+    lengths = blocks.shape
+    return blocks.reshape(*lengths[:dim], lengths[dim] * lengths[dim + 1], *lengths[dim + 2 :])
+
+
+def sent_to_each(value, axis, split_dim, concat_dim):
+    count, here = (lax.axis_size(axis), lax.axis_index(axis))
+    blocks = in_blocks(value, split_dim, count)
+    finished = [blocks[here]]
+    for lap in range(1, count):
+        sent = blocks[(here + lap) % count]
+        finished.append(lax.ppermute(sent, axis, [(i, (i + lap) % count) for i in range(count)]))
+    blocks = jnp.stack(finished)[(here - jnp.arange(count)) % count]
+    return in_order(blocks, concat_dim)
 
 
 def swapped(x, axis, stride):
@@ -118,7 +140,7 @@
     outgoing = jnp.einsum("ks,kcp->scp", select, value, preferred_element_type=jnp.float32).astype(
         jnp.bfloat16
     )
-    incoming = lax.all_to_all(outgoing, "acq", split_axis=0, concat_axis=0, tiled=True)
+    incoming = sent_to_each(outgoing, "acq", 0, 0)
     return incoming[None]
 
 

time: 392 us -> 392 us (level)
  blocking collectives: 139 us -> 131 us
    all_to_all x1 -> x0, blocking collectives: 8.18 us -> none  [shards(): lax.all_to_all(outgoing, 'acq', split_axis=0, concat_axis=0, tiled=True)]
  transfers between devices with their start and end apart: 2 -> 5, of which waited for: 2 -> 5; matrix products, arithmetic and copies ran while one was open for 2% -> 2% of each run, Pallas kernels for 0% -> 0%
where the time goes in v1:
time: 392 us; the launch traced here: 391 us
  blocking collectives  131 us (33%)
  waiting for transfers between devices  108 us (28%)
  local copies, waits for them, and re-layouts  96.6 us (25%)
  other arithmetic  34.8 us (9%)
  matrix products  13.3 us (3%)
  starting transfers between devices  6.32 us (2%)
    psum x1, blocking collectives, shards(): lax.psum(jnp.sum(local_looked[:, 0] ** 2 + local_looked[:, 1] ** 2, axis=...  131 us
    ppermute x2, waiting for transfers between devices, swapped(): lax.ppermute(x, axis, [(i, i ^ 1 << stride) for i in range(lax.axis_size(...  105 us
    another operation x4, local copies, waits for them, and re-layouts, cross_looks(): stacked = jnp.stack([real_part, imag_part], axis=1)  85.9 us
    reduce_sum x2, other arithmetic, cross_looks(): return jnp.sum(stacked, axis=(3, 5)) / (LOOK_L * LOOK_S)  25.5 us
  transfers between devices with their start and end apart: 5, of which 5 were waited for; matrix products, arithmetic and copies ran while one was open for 2% of the time, Pallas kernels for 0%

profile of v1, /device:TPU:2, one launch (start us, length us, event | category | flops | bytes accessed | tf_op | source)
XLA Modules:
  0.0 391.0 jit_solution(140049365928203287)
XLA Ops:
  0.0 2.1 collective-permute-start.1
  2.1 1.4 collective-permute-start
  3.6 0.7 convert_element_type.142
  4.8 1.3 reduce.5
  6.7 0.8 fusion.244
  7.8 53.8 %collective-permute-done.1 = bf16[4,2,128,1280]{3,2,1,0:T(8,128)(2,1)} collective-permute-done((bf16[4,2,128,1280]{3,2,1,0:T(8,128)(2,1)}, bf16[4,2,128,1280]{3,2,1,0:T(8,128)(2,1)}, u32[]{:S(2)}, u32[]{:S(2)}) %collective-permute-start.1) | collective-permute-done | bytes 2621472 | tf_op jit(solution)/shard_map/ppermute | solution.py:38
  61.6 2.5 gather_fusion.2
  64.0 1.8 broadcast_select_fusion
  65.9 50.8 %collective-permute-done = bf16[4,2,128,1280]{3,2,1,0:T(8,128)(2,1)} collective-permute-done((bf16[4,2,128,1280]{3,2,1,0:T(8,128)(2,1)}, bf16[4,2,128,1280]{3,2,1,0:T(8,128)(2,1)}, u32[]{:S(2)}, u32[]{:S(2)}) %collective-permute-start) | collective-permute-done | bytes 2621472 | tf_op jit(solution)/shard_map/ppermute | solution.py:38
  116.6 2.5 gather_fusion.1
  119.4 1.4 copy-done
  120.8 0.8 copy-done.1
  121.6 4.0 %fusion = (f32[4,1,128,1280]{3,2,1,0:T(8,128)}, f32[4,1,128,1280]{3,2,1,0:T(8,128)}, f32[4,1,128,1280]{3,2,1,0:T(8,128)S(1)}, f32[4,1,128,1280]{3,2,1,0:T(8,128)}) fusion(bf16[4,2,128,1280]{3,2,1,0:T(8,128)(2,1)S(1)} %broadcast_select_fusion.1, bf16[4,2,128,1280]{3,2,1,0:T(8,128)(2,1)S(1)} %copy-done.1, bf16[4,2,128,1280]{3,2,1,0:T(8,128)(2,1)S(1)} %copy-done), kind=kLoop, calls=%fused_computation.13 | loop fusion | flops 11796480 | bytes 18350080 | tf_op jit(solution)/shard_map/add | solution.py:71
  125.6 21.7 %stack.51 = f32[4,1,32,4,64,20]{5,4,3,2,0,1:T(8,128)} reshape(f32[4,1,128,1280]{3,2,1,0:T(8,128)} %get-tuple-element.12) | data formatting | bytes 5242880 | tf_op jit(solution)/shard_map/stack | solution.py:73
  147.3 21.7 %stack.52 = f32[4,1,32,4,64,20]{5,4,3,2,0,1:T(8,128)} reshape(f32[4,1,128,1280]{3,2,1,0:T(8,128)} %get-tuple-element.13) | data formatting | bytes 5242880 | tf_op jit(solution)/shard_map/stack | solution.py:73
  168.9 12.7 %maximum_reduce_fusion = f32[4,2,32,64]{3,2,0,1:T(8,128)S(1)} fusion(f32[4,1,32,4,64,20]{5,4,3,2,0,1:T(8,128)} %stack.52, f32[4,1,32,4,64,20]{5,4,3,2,0,1:T(8,128)} %stack.51), kind=kLoop, calls=%fused_computation.3 | loop fusion | flops 2605056 | bytes 5308416 | tf_op jit(solution)/shard_map/reduce_sum | solution.py:77
  185.0 21.7 %stack.57 = f32[4,1,32,4,64,20]{5,4,3,2,0,1:T(8,128)} reshape(f32[4,1,128,1280]{3,2,1,0:T(8,128)} %get-tuple-element.17) | data formatting | bytes 5242880 | tf_op jit(solution)/shard_map/stack | solution.py:73
  206.7 20.9 %stack.58 = f32[4,1,32,4,64,20]{5,4,3,2,0,1:T(8,128)} reshape(f32[4,1,128,1280]{3,2,1,0:T(8,128)S(1)} %get-tuple-element.16) | data formatting | bytes 5242880 | tf_op jit(solution)/shard_map/stack | solution.py:73
  227.6 12.7 %maximum_reduce_fusion.1 = f32[4,2,32,64]{3,2,0,1:T(8,128)S(1)} fusion(f32[4,1,32,4,64,20]{5,4,3,2,0,1:T(8,128)} %stack.58, f32[4,1,32,4,64,20]{5,4,3,2,0,1:T(8,128)} %stack.57), kind=kLoop, calls=%fused_computation.4 | loop fusion | flops 2605056 | bytes 5308416 | tf_op jit(solution)/shard_map/reduce_sum | solution.py:77
  240.5 131.1 %all-reduce = (f32[4]{0:T(128)S(1)}, f32[4]{0:T(128)S(1)}) all-reduce(f32[4]{0:T(128)S(1)} %get-tuple-element.25, f32[4]{0:T(128)S(1)} %get-tuple-element.23), channel_id=1, replica_groups=mesh['acq'=4,'tile'=64] {'tile'}, use_global_device_ids=true, to_apply=%region_7.9 | all-reduce | flops 8 | bytes 64 | tf_op jit(solution)/shard_map/psum | solution.py:104
  371.6 0.5 fusion.60
  376.9 0.5 fusion.9
  377.8 0.5 fusion.8
  379.8 0.5 fusion.5
  380.7 0.5 fusion.4
  383.0 0.6 collective-permute-start.2
  383.6 2.1 collective-permute-start.3
  385.8 1.2 collective-permute-done.2
  387.0 2.0 collective-permute-done.3
  389.0 0.6 collective-permute-done.4
  389.7 0.6 gather_fusion
  390.3 0.8 copy.171
  (65 shorter events, 13.8 us)
Async XLA Ops:
  0.0 61.6 %collective-permute-start.1 = (bf16[4,2,128,1280]{3,2,1,0:T(8,128)(2,1)}, bf16[4,2,128,1280]{3,2,1,0:T(8,128)(2,1)}, u32[]{:S(2)}, u32[]{:S(2)}) collective-permute-start(bf16[4,2,128,1280]{3,2,1,0:T(8,128)(2,1)} %param.6), channel_id=1, source_target_pairs={{0,128},{64,192},{128,0},{192,64},{1,129},{65,193},{129,1},{193,65... | collective-permute-start | bytes 7864328 | tf_op jit(solution)/shard_map/ppermute | solution.py:38
  2.1 114.5 %collective-permute-start = (bf16[4,2,128,1280]{3,2,1,0:T(8,128)(2,1)}, bf16[4,2,128,1280]{3,2,1,0:T(8,128)(2,1)}, u32[]{:S(2)}, u32[]{:S(2)}) collective-permute-start(bf16[4,2,128,1280]{3,2,1,0:T(8,128)(2,1)} %param.6), channel_id=1, source_target_pairs={{0,64},{64,0},{128,192},{192,128},{1,65},{65,1},{129,193},{193,129... | collective-permute-start | bytes 7864328 | tf_op jit(solution)/shard_map/ppermute | solution.py:38
  119.1 1.7 copy-start
  119.1 2.5 copy-start.1
  383.0 4.0 %collective-permute-start.2 = (bf16[64,2,128]{2,0,1:T(8,128)(2,1)S(1)}, bf16[64,2,128]{2,0,1:T(8,128)(2,1)S(1)}, u32[]{:S(2)}, u32[]{:S(2)}) collective-permute-start(bf16[64,2,128]{2,0,1:T(8,128)(2,1)S(1)} %get-tuple-element.21), channel_id=1, source_target_pairs={{0,64},{64,128},{128,192},{192,0},{1,65},{65,129},{129,193},{193,1... | collective-permute-start | bytes 98312 | tf_op jit(solution)/shard_map/ppermute | solution.py:32
  383.6 5.4 %collective-permute-start.3 = (bf16[64,2,128]{2,0,1:T(8,128)(2,1)S(1)}, bf16[64,2,128]{2,0,1:T(8,128)(2,1)S(1)}, u32[]{:S(2)}, u32[]{:S(2)}) collective-permute-start(bf16[64,2,128]{2,0,1:T(8,128)(2,1)S(1)} %get-tuple-element.20), channel_id=1, source_target_pairs={{0,128},{64,192},{128,0},{192,64},{1,129},{65,193},{129,1},{193,65... | collective-permute-start | bytes 98312 | tf_op jit(solution)/shard_map/ppermute | solution.py:32
  385.7 3.9 %collective-permute-start.4 = (bf16[64,2,128]{2,0,1:T(8,128)(2,1)S(1)}, bf16[64,2,128]{2,0,1:T(8,128)(2,1)S(1)}, u32[]{:S(2)}, u32[]{:S(2)}) collective-permute-start(bf16[64,2,128]{2,0,1:T(8,128)(2,1)S(1)} %get-tuple-element.19), channel_id=1, source_target_pairs={{0,192},{64,0},{128,64},{192,128},{1,193},{65,1},{129,65},{193,129... | collective-permute-start | bytes 98312 | tf_op jit(solution)/shard_map/ppermute | solution.py:32
